TPU v7x, 256 devices: a whole 4x4x8 slice. The times are simulated.
256 devices in a mesh: pipe: 8 (over z_lo, core), ep: 32 (over x, y, z_hi).
Axes of the slice: x: 4, y: 4, z: 8 (z_hi: 2, z_lo: 4; z = z_hi * 4 + z_lo), core: 2. Of those that a mesh axis runs over, the one named last changes fastest.
Arguments:
- x_fwd: bfloat16 [8, 2048, 2048], P('pipe', 'ep'), may hold values from -6 to 6
- ids_fwd: int32 [8, 2048, 8], P('pipe', 'ep'), may hold values from 0 to 31, all different within a row; in each aligned block of 64 rows (0 to 63, 64 to 127, ..., all dimensions but the last counted through in order) at most 24 rows name the same one
- route_fwd: float32 [8, 2048, 8], P('pipe', 'ep'), may hold values from 0.05 to 1
- x_bwd: bfloat16 [8, 2048, 2048], P('pipe', 'ep'), may hold values from -6 to 6
- grad_bwd: bfloat16 [8, 2048, 2048], P('pipe', 'ep'), may hold values from -6 to 6
- ids_bwd: int32 [8, 2048, 8], P('pipe', 'ep'), may hold values from 0 to 31, all different within a row; in each aligned block of 64 rows (0 to 63, 64 to 127, ..., all dimensions but the last counted through in order) at most 24 rows name the same one
- route_bwd: float32 [8, 2048, 8], P('pipe', 'ep'), may hold values from 0.05 to 1
- norm_gain: bfloat16 [8, 2048], P('pipe'), may hold values from 0.25 to 1.75
- w_gate: bfloat16 [8, 32, 2048, 768], P('pipe', 'ep'), may hold values from -0.125 to 0.125
- w_up: bfloat16 [8, 32, 2048, 768], P('pipe', 'ep'), may hold values from -0.125 to 0.125
- w_down: bfloat16 [8, 32, 768, 2048], P('pipe', 'ep'), may hold values from -0.21875 to 0.21875
Outputs:
- fwd_next: bfloat16 [8, 2048, 2048], P('pipe', 'ep')
- bwd_prev: bfloat16 [8, 2048, 2048], P('pipe', 'ep')
Inputs may be any that keep to these rules, and one draw needn't show every extreme that they name: `ids_fwd`: in each aligned block of 64 tokens of a section, each token names 8 different experts, no expert is named by more than 24 tokens, and in some block one expert is named by exactly 24. `ids_bwd`: as for ids_fwd.
All inputs are finite; a program needn't handle non-finite values.
Results may differ from a plain program's by a relative error of at most 0.0046.
Values may be sent and summed in bfloat16 or wider, within the bound.
A program may use at most 128 MiB of HBM per device.

v0:
```python
import jax
import jax.numpy as jnp
from jax import lax
from jax.sharding import PartitionSpec as P

EPS = 1e-06


def from_behind(block, axis, distance):
    devices = range(lax.axis_size(axis))
    route = [((i - distance) % len(devices), i) for i in devices]
    return lax.ppermute(block, axis, route)


def slot_places(ids, n_exp, cap):
    flat = ids.reshape(-1)
    onehot = (flat[:, None] == jnp.arange(n_exp, dtype=jnp.int32)[None, :]).astype(jnp.int32)
    before = jnp.cumsum(onehot, axis=0) - onehot
    slot = jnp.sum(before * onehot, axis=1)
    return flat * cap + slot


def rms_stats(x):
    xf = x.astype(jnp.float32)
    scale = lax.rsqrt(jnp.mean(xf * xf, axis=-1, keepdims=True) + EPS)
    return (xf, scale)


def expert_forward(rows, w_g, w_u, w_d):
    gate = jnp.dot(rows, w_g, preferred_element_type=jnp.float32)
    upper = jnp.dot(rows, w_u, preferred_element_type=jnp.float32)
    act = (jax.nn.silu(gate) * upper).astype(jnp.bfloat16)
    return jnp.dot(act, w_d, preferred_element_type=jnp.float32).astype(jnp.bfloat16)


def expert_backward(rows, cot, w_g, w_u, w_d):
    gate = jnp.dot(rows, w_g, preferred_element_type=jnp.float32)
    upper = jnp.dot(rows, w_u, preferred_element_type=jnp.float32)
    sigma = jax.nn.sigmoid(gate)
    dact = jnp.dot(cot, w_d.T, preferred_element_type=jnp.float32)
    dgate = (dact * upper * sigma * (1.0 + gate * (1.0 - sigma))).astype(jnp.bfloat16)
    dup = (dact * gate * sigma).astype(jnp.bfloat16)
    total = jnp.dot(dgate, w_g.T, preferred_element_type=jnp.float32) + jnp.dot(
        dup, w_u.T, preferred_element_type=jnp.float32
    )
    return total.astype(jnp.bfloat16)


def norm_backward(xf, scale, gain, upstream):
    scaled = gain * upstream
    inner = jnp.mean(xf * scaled, axis=-1, keepdims=True)
    return scale * scaled - xf * (scale * scale * scale) * inner


def route_layout(ids, route, n_exp, cap):
    top = ids.shape[1]
    places = slot_places(ids, n_exp, cap)
    count = places.shape[0]
    source = (
        jnp.full((n_exp * cap,), -1, jnp.int32).at[places].set(jnp.arange(count, dtype=jnp.int32))
    )
    valid = (source >= 0)[:, None]
    safe = jnp.maximum(source, 0)
    weights = route / jnp.sum(route, axis=-1, keepdims=True)
    return (places, valid, safe // top, weights.reshape(-1)[safe], weights)


def local(
    x_fwd, ids_fwd, route_fwd, x_bwd, grad_bwd, ids_bwd, route_bwd, norm_gain, w_gate, w_up, w_down
):
    n_exp = lax.axis_size("ep")
    tok_dev = x_fwd.shape[1]
    width = x_fwd.shape[2]
    top = ids_fwd.shape[2]
    cap = 3 * tok_dev * top // (2 * n_exp)
    gain = norm_gain[0].astype(jnp.float32)
    w_g = w_gate[0, 0]
    w_u = w_up[0, 0]
    w_d = w_down[0, 0]
    zero_b = jnp.zeros((), jnp.bfloat16)
    xf, scale_f = rms_stats(x_fwd[0])
    h_f = (xf * scale_f * gain).astype(jnp.bfloat16)
    xb, scale_b = rms_stats(x_bwd[0])
    h_b = (xb * scale_b * gain).astype(jnp.bfloat16)
    grad = grad_bwd[0]
    places_f, valid_f, token_f, slot_w_f, weights_f = route_layout(
        ids_fwd[0], route_fwd[0], n_exp, cap
    )
    places_b, valid_b, token_b, slot_w_b, weights_b = route_layout(
        ids_bwd[0], route_bwd[0], n_exp, cap
    )
    send_f = jnp.where(valid_f, h_f[token_f], zero_b).reshape(n_exp, cap, width)
    send_b = jnp.where(valid_b, h_b[token_b], zero_b).reshape(n_exp, cap, width)
    cot_rows = (slot_w_b[:, None] * grad[token_b].astype(jnp.float32)).astype(jnp.bfloat16)
    send_g = jnp.where(valid_b, cot_rows, zero_b).reshape(n_exp, cap, width)
    got_f, got_b, got_g = (
        lax.all_to_all(send_f, "ep", split_axis=0, concat_axis=0, tiled=True),
        lax.all_to_all(send_b, "ep", split_axis=0, concat_axis=0, tiled=True),
        lax.all_to_all(send_g, "ep", split_axis=0, concat_axis=0, tiled=True),
    )
    rows = got_f.reshape(-1, width)
    made_f = expert_forward(rows, w_g, w_u, w_d).reshape(got_f.shape)
    rows = got_b.reshape(-1, width)
    cots = got_g.reshape(-1, width)
    made_b = expert_backward(rows, cots, w_g, w_u, w_d).reshape(got_b.shape)
    back_f, back_b = (
        lax.all_to_all(made_f, "ep", split_axis=0, concat_axis=0, tiled=True),
        lax.all_to_all(made_b, "ep", split_axis=0, concat_axis=0, tiled=True),
    )
    picked_f = back_f.reshape(-1, width)[places_f].reshape(tok_dev, top, width)
    mixed = jnp.sum(weights_f[:, :, None] * picked_f.astype(jnp.float32), axis=1)
    layer_out = (xf + mixed).astype(jnp.bfloat16)[None]
    picked_b = back_b.reshape(-1, width)[places_b].reshape(tok_dev, top, width)
    dnorm = jnp.sum(picked_b.astype(jnp.float32), axis=1)
    input_grad = (grad.astype(jnp.float32) + norm_backward(xb, scale_b, gain, dnorm)).astype(
        jnp.bfloat16
    )[None]
    fwd_next = from_behind(layer_out, "pipe", 1)
    bwd_prev = from_behind(input_grad, "pipe", -1)
    return (fwd_next, bwd_prev)


def solution(mesh):
    placed = (
        P("pipe", "ep", None),
        P("pipe", "ep", None),
        P("pipe", "ep", None),
        P("pipe", "ep", None),
        P("pipe", "ep", None),
        P("pipe", "ep", None),
        P("pipe", "ep", None),
        P("pipe", None),
        P("pipe", "ep", None, None),
        P("pipe", "ep", None, None),
        P("pipe", "ep", None, None),
    )
    return jax.shard_map(
        local,
        mesh=mesh,
        in_specs=placed,
        out_specs=(P("pipe", "ep", None), P("pipe", "ep", None)),
        check_vma=False,
    )
```

profile of v0, /device:TPU:1, one launch (start us, length us, event | category | flops | bytes accessed | tf_op | source)
XLA Modules:
  0.0 482.4 jit_solution(16723587907577652183)
XLA Ops:
  10.8 8.2 %gather_fusion.4 = bf16[768,2048]{1,0:T(8,128)(2,1)} fusion(bf16[64,2048]{1,0:T(8,128)(2,1)} %fusion.37, s32[1024]{0:T(1024)S(1)} %get-tuple-element.10), kind=kCustom, calls=%fused_computation.4 | custom fusion | bytes 6294528 | tf_op jit(solution)/shard_map/gather | solution.py:93
  19.0 4.3 gather_fusion.3
  23.7 5.0 %gather_fusion.2 = f32[768]{0:T(1024)S(1)} fusion(f32[512]{0:T(512)S(1)} %div.60, s32[1024]{0:T(1024)S(1)} %get-tuple-element.11), kind=kCustom, calls=%fused_computation.2 | custom fusion | bytes 9216 | tf_op jit(solution)/shard_map/gather | solution.py:65
  28.9 5.1 %fusion.2 = (bf16[32,24,2048]{2,1,0:T(8,128)(2,1)}, bf16[32,24,2048]{2,1,0:T(8,128)(2,1)S(1)}) fusion(bf16[32,24,2048]{2,1,0:T(8,128)(2,1)} %bitcast.133, f32[32,24]{1,0:T(8,128)S(1)} %mul.206, pred[32,24]{1,0:T(8,128)(4,1)S(1)} %broadcast_in_dim.60, bf16[32,24,2048]{2,1,0:T(8,128)(2,1)} %bitcast.132), kind=kLoop, calls=%fused_computation.15 | loop fusion | flops 7864320 | bytes 12586752 | tf_op jit(solution)/shard_map/jit(_where)/select_n | solution.py:95
  34.0 69.1 %all_to_all.25 = bf16[32,24,2048]{2,1,0:T(8,128)(2,1)} all-to-all(bf16[32,24,2048]{2,1,0:T(8,128)(2,1)S(1)} %get-tuple-element.5), channel_id=1, replica_groups=mesh['pipe'=8,'ep'=32] {'ep'}, dimensions={0} | all-to-all | bytes 6291456 | tf_op jit(solution)/shard_map/all_to_all | solution.py:98
  103.1 5.1 %all-to-all-start.2 = ((bf16[32,24,2048]{2,1,0:T(8,128)(2,1)}), bf16[32,24,2048]{2,1,0:T(8,128)(2,1)}, u32[]{:S(2)}, u32[]{:S(2)}) async-start(bf16[32,24,2048]{2,1,0:T(8,128)(2,1)} %get-tuple-element.4), calls=%async_computation.2 | async-start | bytes 6291456 | tf_op jit(solution)/shard_map/all_to_all | solution.py:99
  108.3 6.8 %fusion.13 = f32[768,768]{1,0:T(8,128)} fusion(bf16[768,2048]{1,0:T(8,128)(2,1)} %bitcast.137, bf16[1,1,2048,768]{3,2,1,0:T(8,128)(2,1)} %param.19), kind=kOutput, calls=%fused_computation.26 | convolution fusion | flops 2415919104 | bytes 8650752 | tf_op jit(solution)/shard_map/dot_general | solution.py:37
  115.1 28.2 %all-to-all-done.2 = bf16[32,24,2048]{2,1,0:T(8,128)(2,1)} async-done(((bf16[32,24,2048]{2,1,0:T(8,128)(2,1)}), bf16[32,24,2048]{2,1,0:T(8,128)(2,1)}, u32[]{:S(2)}, u32[]{:S(2)}) %all-to-all-start.2) | async-done | bytes 3145760 | tf_op jit(solution)/shard_map/all_to_all | solution.py:99
  143.3 7.0 %fusion.3 = f32[768,768]{1,0:T(8,128)} fusion(bf16[768,2048]{1,0:T(8,128)(2,1)} %bitcast.21, bf16[1,1,768,2048]{3,2,1,0:T(8,128)(2,1)} %param.21), kind=kOutput, calls=%fused_computation.16 | convolution fusion | flops 2415919104 | bytes 8650752 | tf_op jit(solution)/shard_map/dot_general | solution.py:40
  150.3 12.7 %fusion.11 = f32[768,2048]{1,0:T(8,128)} fusion(bf16[1,1,2048,768]{3,2,1,0:T(8,128)(2,1)} %param.19, f32[768,768]{1,0:T(8,128)} %fusion.13, f32[768,768]{1,0:T(8,128)} %fusion.3, bf16[768,2048]{1,0:T(8,128)(2,1)} %bitcast.138, bf16[1,1,2048,768]{3,2,1,0:T(8,128)(2,1)S(1)} %copy-done), kind=kOutput, calls=%fused_computation.24 | convolution fusion | flops 4837736448 | bytes 20447232 | tf_op jit(solution)/shard_map/dot_general | solution.py:43
  163.0 7.5 %add_convert_fusion = bf16[768,2048]{1,0:T(8,128)(2,1)} fusion(f32[768,2048]{1,0:T(8,128)} %fusion.11, bf16[1,1,2048,768]{3,2,1,0:T(8,128)(2,1)S(1)} %copy-done, f32[768,768]{1,0:T(8,128)} %fusion.3, f32[768,768]{1,0:T(8,128)} %fusion.13), kind=kOutput, calls=%fused_computation.10 | convolution fusion | flops 2422603776 | bytes 17301504 | tf_op jit(solution)/shard_map/dot_general | solution.py:43
  170.5 14.3 %all-to-all-start.4 = ((bf16[32,24,2048]{2,1,0:T(8,128)(2,1)}), bf16[32,24,2048]{2,1,0:T(8,128)(2,1)}, u32[]{:S(2)}, u32[]{:S(2)}) async-start(bf16[32,24,2048]{2,1,0:T(8,128)(2,1)} %bitcast.135), calls=%async_computation.4 | async-start | bytes 6291456 | tf_op jit(solution)/shard_map/all_to_all | solution.py:108
  192.4 25.7 %all-to-all-done.4 = bf16[32,24,2048]{2,1,0:T(8,128)(2,1)} async-done(((bf16[32,24,2048]{2,1,0:T(8,128)(2,1)}), bf16[32,24,2048]{2,1,0:T(8,128)(2,1)}, u32[]{:S(2)}, u32[]{:S(2)}) %all-to-all-start.4) | async-done | bytes 3145760 | tf_op jit(solution)/shard_map/all_to_all | solution.py:108
  218.0 7.5 %gather_fusion.5 = bf16[512,2048]{1,0:T(8,128)(2,1)} fusion(bf16[768,2048]{1,0:T(8,128)(2,1)} %bitcast.25, s32[1024]{0:T(1024)S(1)} %pad_clamp_fusion), kind=kCustom, calls=%fused_computation.5 | custom fusion | bytes 4196352 | tf_op jit(solution)/shard_map/gather | solution.py:113
  231.4 8.1 %gather_fusion = bf16[768,2048]{1,0:T(8,128)(2,1)} fusion(bf16[64,2048]{1,0:T(8,128)(2,1)} %get-tuple-element.3, s32[1024]{0:T(1024)S(1)} %pad_clamp_fusion.4), kind=kCustom, calls=%fused_computation | custom fusion | bytes 6294528 | tf_op jit(solution)/shard_map/gather | solution.py:92
  241.7 72.0 %all_to_all.26 = bf16[32,24,2048]{2,1,0:T(8,128)(2,1)S(1)} all-to-all(bf16[32,24,2048]{2,1,0:T(8,128)(2,1)S(1)} %broadcast_select_fusion.1), channel_id=1, replica_groups=mesh['pipe'=8,'ep'=32] {'ep'}, dimensions={0} | all-to-all | bytes 6291456 | tf_op jit(solution)/shard_map/all_to_all | solution.py:97
  315.4 4.0 fusion.9
  319.4 11.9 %convolution_convert_fusion = bf16[768,2048]{1,0:T(8,128)(2,1)} fusion(bf16[1,1,768,2048]{3,2,1,0:T(8,128)(2,1)} %param.21, f32[768,768]{1,0:T(8,128)} %fusion.9, bf16[768,2048]{1,0:T(8,128)(2,1)} %bitcast.140, bf16[1,1,2048,768]{3,2,1,0:T(8,128)(2,1)} %param.19), kind=kOutput, calls=%fused_computation.14 | convolution fusion | flops 4836950016 | bytes 14942208 | tf_op jit(solution)/shard_map/dot_general | solution.py:33
  331.3 5.0 %all-to-all-start.1 = ((bf16[32,24,2048]{2,1,0:T(8,128)(2,1)}), bf16[32,24,2048]{2,1,0:T(8,128)(2,1)}, u32[]{:S(2)}, u32[]{:S(2)}) async-start(bf16[32,24,2048]{2,1,0:T(8,128)(2,1)} %bitcast.136), calls=%async_computation.1 | async-start | bytes 6291456 | tf_op jit(solution)/shard_map/all_to_all | solution.py:107
  338.5 28.5 %collective-permute-start.1 = (bf16[1,64,2048]{2,1,0:T(8,128)(2,1)}, bf16[1,64,2048]{2,1,0:T(8,128)(2,1)}, u32[]{:S(2)}, u32[]{:S(2)}) collective-permute-start(bf16[1,64,2048]{2,1,0:T(8,128)(2,1)} %fusion.42), channel_id=1, source_target_pairs={{32,0},{64,32},{96,64},{128,96},{160,128},{192,160},{224,192},{0,2... | collective-permute-start | bytes 786440 | tf_op jit(solution)/shard_map/ppermute | solution.py:12
  367.1 7.6 %gather_fusion.1 = bf16[512,2048]{1,0:T(8,128)(2,1)} fusion(bf16[768,2048]{1,0:T(8,128)(2,1)} %bitcast.12, s32[1024]{0:T(1024)S(1)} %pad_clamp_fusion.3), kind=kCustom, calls=%fused_computation.1 | custom fusion | bytes 4196352 | tf_op jit(solution)/shard_map/gather | solution.py:110
  374.7 3.4 fusion.1
  378.2 98.2 %collective-permute-start = (bf16[1,64,2048]{2,1,0:T(8,128)(2,1)S(1)}, bf16[1,64,2048]{2,1,0:T(8,128)(2,1)S(1)}, u32[]{:S(2)}, u32[]{:S(2)}) collective-permute-start(bf16[1,64,2048]{2,1,0:T(8,128)(2,1)S(1)} %fusion.34), channel_id=1, source_target_pairs={{224,0},{0,32},{32,64},{64,96},{96,128},{128,160},{160,192},{192,2... | collective-permute-start | bytes 786440 | tf_op jit(solution)/shard_map/ppermute | solution.py:12
  476.4 3.3 collective-permute-done
  (88 shorter events, 32.5 us)
Async XLA Ops:
  0.6 149.7 %copy-start = (bf16[1,1,2048,768]{3,2,1,0:T(8,128)(2,1)S(1)}, bf16[1,1,2048,768]{3,2,1,0:T(8,128)(2,1)}, u32[]{:S(2)}) copy-start(bf16[1,1,2048,768]{3,2,1,0:T(8,128)(2,1)} %param.20) | copy-start | bytes 9437188
  9.0 10.0 %copy-start.8 = (f32[64]{0:T(128)}, f32[64]{0:T(128)S(1)}, u32[]{:S(2)}) copy-start(f32[64]{0:T(128)S(1)} %get-tuple-element.9) | copy-start | bytes 772
  10.8 8.2 %copy-start.1 = (bf16[1,64,2048]{2,1,0:T(8,128)(2,1)S(1)}, bf16[1,64,2048]{2,1,0:T(8,128)(2,1)}, u32[]{:S(2)}) copy-start(bf16[1,64,2048]{2,1,0:T(8,128)(2,1)} %param.15) | copy-start | bytes 786436
  19.0 4.3 copy-start.5
  103.1 40.2 %all-to-all-start.2 = ((bf16[32,24,2048]{2,1,0:T(8,128)(2,1)}), bf16[32,24,2048]{2,1,0:T(8,128)(2,1)}, u32[]{:S(2)}, u32[]{:S(2)}) async-start(bf16[32,24,2048]{2,1,0:T(8,128)(2,1)} %get-tuple-element.4), calls=%async_computation.2 | async-start | bytes 6291456 | tf_op jit(solution)/shard_map/all_to_all | solution.py:99
  170.5 14.3 %copy-start.6 = (s32[1,64,8]{1,2,0:T(8,128)S(1)}, s32[1,64,8]{1,2,0:T(8,128)}, u32[]{:S(2)}) copy-start(s32[1,64,8]{1,2,0:T(8,128)} %param.12) | copy-start | bytes 6148
  170.5 47.5 %all-to-all-start.4 = ((bf16[32,24,2048]{2,1,0:T(8,128)(2,1)}), bf16[32,24,2048]{2,1,0:T(8,128)(2,1)}, u32[]{:S(2)}, u32[]{:S(2)}) async-start(bf16[32,24,2048]{2,1,0:T(8,128)(2,1)} %bitcast.135), calls=%async_computation.4 | async-start | bytes 6291456 | tf_op jit(solution)/shard_map/all_to_all | solution.py:108
  228.6 0.8 copy-start.2
  313.7 1.7 copy-start.3
  331.3 5.0 %copy-start.7 = (f32[1,64,8]{1,2,0:T(8,128)S(1)}, f32[1,64,8]{1,2,0:T(8,128)}, u32[]{:S(2)}) copy-start(f32[1,64,8]{1,2,0:T(8,128)} %param.13) | copy-start | bytes 6148
  331.3 5.1 %copy-start.9 = (f32[64]{0:T(128)S(1)}, f32[64]{0:T(128)}, u32[]{:S(2)}) copy-start(f32[64]{0:T(128)} %copy-done.8) | copy-start | bytes 772
  331.3 5.1 %copy-start.10 = (f32[64]{0:T(128)S(1)}, f32[64]{0:T(128)}, u32[]{:S(2)}) copy-start(f32[64]{0:T(128)} %get-tuple-element.8) | copy-start | bytes 772
  331.3 35.7 %all-to-all-start.1 = ((bf16[32,24,2048]{2,1,0:T(8,128)(2,1)}), bf16[32,24,2048]{2,1,0:T(8,128)(2,1)}, u32[]{:S(2)}, u32[]{:S(2)}) async-start(bf16[32,24,2048]{2,1,0:T(8,128)(2,1)} %bitcast.136), calls=%async_computation.1 | async-start | bytes 6291456 | tf_op jit(solution)/shard_map/all_to_all | solution.py:107
  338.5 137.9 %collective-permute-start.1 = (bf16[1,64,2048]{2,1,0:T(8,128)(2,1)}, bf16[1,64,2048]{2,1,0:T(8,128)(2,1)}, u32[]{:S(2)}, u32[]{:S(2)}) collective-permute-start(bf16[1,64,2048]{2,1,0:T(8,128)(2,1)} %fusion.42), channel_id=1, source_target_pairs={{32,0},{64,32},{96,64},{128,96},{160,128},{192,160},{224,192},{0,2... | collective-permute-start | bytes 786440 | tf_op jit(solution)/shard_map/ppermute | solution.py:12
  367.1 11.1 %copy-start.4 = (bf16[1,64,2048]{2,1,0:T(8,128)(2,1)S(1)}, bf16[1,64,2048]{2,1,0:T(8,128)(2,1)}, u32[]{:S(2)}) copy-start(bf16[1,64,2048]{2,1,0:T(8,128)(2,1)} %param.11) | copy-start | bytes 786436
  378.2 101.5 %collective-permute-start = (bf16[1,64,2048]{2,1,0:T(8,128)(2,1)S(1)}, bf16[1,64,2048]{2,1,0:T(8,128)(2,1)S(1)}, u32[]{:S(2)}, u32[]{:S(2)}) collective-permute-start(bf16[1,64,2048]{2,1,0:T(8,128)(2,1)S(1)} %fusion.34), channel_id=1, source_target_pairs={{224,0},{0,32},{32,64},{64,96},{96,128},{128,160},{160,192},{192,2... | collective-permute-start | bytes 786440 | tf_op jit(solution)/shard_map/ppermute | solution.py:12
where the time goes:
time: 489 us; the launch traced here: 482 us
  starting transfers between devices  151 us (31%)
  blocking collectives  141 us (29%)
  waiting for transfers between devices  57.2 us (12%)
  local copies, waits for them, and re-layouts  54.6 us (11%)
  matrix products  49.9 us (10%)
  other arithmetic  27.2 us (6%)
    ppermute x2, starting transfers between devices, from_behind(): return lax.ppermute(block, axis, route)  127 us
    all_to_all x1, blocking collectives, local(): lax.all_to_all(send_f, 'ep', split_axis=0, concat_axis=0, tiled=True)  72 us
    all_to_all x1, blocking collectives, local(): lax.all_to_all(send_b, 'ep', split_axis=0, concat_axis=0, tiled=True)  69.1 us
    all_to_all x1, waiting for transfers between devices, local(): lax.all_to_all(send_g, 'ep', split_axis=0, concat_axis=0, tiled=True)  28.2 us
    all_to_all x1, waiting for transfers between devices, local(): lax.all_to_all(made_b, 'ep', split_axis=0, concat_axis=0, tiled=True)  25.7 us
    all_to_all x1, starting transfers between devices, local(): lax.all_to_all(made_b, 'ep', split_axis=0, concat_axis=0, tiled=True)  14.3 us
    dot_general x1, matrix products, expert_backward(): jnp.dot(dgate, w_g.T, preferred_element_type=jnp.float32)  12.7 us
    dot_general x1, matrix products, expert_forward(): jnp.dot(act, w_d, preferred_element_type=jnp.float32).astype(jnp.bfloat16)  11.9 us
  transfers between devices with their start and end apart: 5, of which 3 were waited for; matrix products, arithmetic and copies ran while one was open for 6% of the time, Pallas kernels for 0%

commit v1 on v0

v1 whole, which is shorter than its diff:
```python
import functools

import jax
import jax.numpy as jnp
from jax import lax
from jax.experimental import pallas as pl
from jax.experimental.pallas import tpu as pltpu
from jax.sharding import PartitionSpec as P

EPS = 1e-06
MESH = pl.DeviceIdType.MESH
F32, BF16 = jnp.float32, jnp.bfloat16

SIDE = 4
TOK = 64
CAP = 24
PAIR = 2 * CAP
D = 2048
HALF = D // 2
FF = 768
TOP = 8
NT = 256
G, HB, HF = 0, 1, 2
FWD, BWD = 0, 1


def dot(a, b):
    return jnp.dot(a, b, preferred_element_type=F32)


def dot_t(a, b):
    return lax.dot_general(a, b, (((1,), (1,)), ((), ())), preferred_element_type=F32)


def kernel(
    xf_ref, idf_ref, rtf_ref, xb_ref, gr_ref, idb_ref, rtb_ref, gain_ref, wg_hbm, wu_hbm, wd_hbm,
    outf_ref, outb_ref,
    wg, wu, wd, dense, pool, slots, ret, part, own, gath, zout, zin, last, act1, act2,
    meta, meta_z, meta_d, sel, sel_t, slot_w,
    w_sem, mz_s, mz_r, ma_s, ma_r, zs, zr, ds_s, ds_r, xs, xr, rs, rr, cs, cr, qs, qr, ps, pr,
):
    p = lax.axis_index("pipe")
    e = lax.axis_index("ep")
    x, y, z = e // 8, lax.rem(e // 2, SIDE), lax.rem(e, 2)

    def at(dx, dy, dz):
        return (p, lax.rem(x + dx, SIDE) * 8 + lax.rem(y + dy, SIDE) * 2 + lax.rem(z + dz, 2))

    def first(q, d):
        return at(0, d, 0) if q == 0 else at(d, 0, 0)

    def second(q, d):
        return first(1 - q, d)

    partner = at(0, 0, 1)
    ahead, behind = (lax.rem(p + 1, 8), e), (lax.rem(p + 7, 8), e)

    def send(src, dst, s, r, device):
        pltpu.make_async_remote_copy(
            src_ref=src, dst_ref=dst, send_sem=s, recv_sem=r, device_id=device, device_id_type=MESH
        ).start()

    def take(ref, sem):
        pltpu.make_async_copy(ref, ref, sem).wait()

    barrier = pltpu.get_barrier_semaphore()
    for device in [partner, ahead, behind] + [first(q, d) for q in (0, 1) for d in (1, 2, 3)]:
        pl.semaphore_signal(barrier, inc=1, device_id=device, device_id_type=MESH)
    loads = [
        pltpu.make_async_copy(src, dst, w_sem.at[i])
        for i, (src, dst) in enumerate(((wg_hbm, wg), (wu_hbm, wu), (wd_hbm, wd)))
    ]
    for load in loads:
        load.start()

    shape = (2 * TOK, 128)
    row = lax.broadcasted_iota(jnp.int32, shape, 1)
    i, d, q, dz = row % 4, (row // 8) % 4, (row // 32) % 2, row // 64
    ex = jnp.where(q == 0, i, d)
    ey = jnp.where(q == 0, d, i)
    expert = ((x + ex) % SIDE) * 8 + ((y + ey) % SIDE) * 2 + (z + dz) % 2
    ids = jnp.concatenate([idf_ref[...], idb_ref[...]], axis=0)
    route = jnp.concatenate([rtf_ref[...], rtb_ref[...]], axis=0)
    route = route / jnp.sum(route, axis=-1, keepdims=True)
    picked = jnp.zeros(shape, F32)
    weight = jnp.zeros(shape, F32)
    for k in range(TOP):
        hit = ids[:, k : k + 1] == expert
        picked = jnp.where(hit, 1.0, picked)
        weight = jnp.where(hit, route[:, k : k + 1], weight)
    picked, weight = picked.T, weight.T
    early = lax.broadcasted_iota(jnp.int32, (128, 128), 0)
    late = lax.broadcasted_iota(jnp.int32, (128, 128), 1)
    order = jnp.where((early < late) & (early // TOK == late // TOK), 1.0, 0.0).astype(BF16)
    before = dot(picked.astype(BF16), order)
    place = jnp.where(picked > 0.0, before, -1000.0)
    kind = (lax.broadcasted_iota(jnp.int32, (128, 128), 0) // 4) % 2
    meta[...] = jnp.where(kind == 0, place, weight).reshape(2, 2, 4, 8, 128)
    pl.semaphore_wait(barrier, 9)

    def send_own(t):
        for q in (0, 1):
            send(dense.at[t, q, 0, 0], dense.at[t, q, 0, 1], zs.at[t, q], zr.at[t, q], partner)
        for q in (0, 1):
            for d in (2, 1, 3):
                there = dense.at[t, q, SIDE - d, 0]
                send(dense.at[t, q, 0, 0], there, ds_s.at[t], ds_r.at[t, q, SIDE - d, 0], first(q, d))

    def send_partners(t):
        for q in (0, 1):
            take(dense.at[t, q, 0, 1], zr.at[t, q])
            for d in (2, 1, 3):
                there = dense.at[t, q, SIDE - d, 1]
                send(dense.at[t, q, 0, 1], there, ds_s.at[t], ds_r.at[t, q, SIDE - d, 1], first(q, d))

    def normed(ref, t):
        v = ref[...].astype(F32)
        scale = lax.rsqrt(jnp.mean(v * v, axis=-1, keepdims=True) + EPS)
        h = (v * scale * gain_ref[...].astype(F32)).astype(BF16)
        for q in (0, 1):
            dense[t, q, 0, 0] = h[:, q * HALF : (q + 1) * HALF]

    send(meta.at[1], meta_z, mz_s, mz_r, partner)
    for q in (0, 1):
        for d in (1, 2, 3):
            send(meta.at[0, q, d], meta_d.at[q, SIDE - d, 0], ma_s, ma_r, first(q, d))
        dense[G, q, 0, 0] = gr_ref[:, q * HALF : (q + 1) * HALF]
    send_own(G)
    normed(xb_ref, HB)
    send_own(HB)
    take(meta_z, mz_r)
    for q in (0, 1):
        for d in (1, 2, 3):
            send(meta_z.at[q, d], meta_d.at[q, SIDE - d, 1], ma_s, ma_r, first(q, d))
        meta_d[q, 0, 0] = meta[0, q, 0]
        meta_d[q, 0, 1] = meta_z[q, 0]
    normed(xf_ref, HF)
    take(meta_d.at[:, 1:4], ma_r)

    lane = lax.broadcasted_iota(jnp.int32, (8, 128), 1)
    slot = lax.broadcasted_iota(jnp.int32, (PAIR, 128), 0).astype(F32)

    @pl.loop(0, 8)
    def _(n):
        q, d = n // 4, lax.rem(n, 4)
        m0, m1 = meta_d[q, d, 0], meta_d[q, d, 1]
        r0, r1 = pltpu.roll(m0, TOK, 1), pltpu.roll(m1, TOK, 1)
        for way, m in ((FWD, jnp.where(lane < TOK, m0, r1)), (BWD, jnp.where(lane < TOK, r0, m1))):
            shifted = m + jnp.where(lane < TOK, 0.0, 1.0 * CAP)
            ones, weighed = [], []
            for i in range(SIDE):
                hit = jnp.broadcast_to(shifted[i : i + 1], (PAIR, 128)) == slot
                ones.append(jnp.where(hit, 1.0, 0.0))
                weighed.append(jnp.where(hit, jnp.broadcast_to(m[4 + i : 5 + i], (PAIR, 128)), 0.0))
            fill = [jnp.zeros((256 - SIDE * PAIR, 128), F32)]
            one = jnp.concatenate(ones, axis=0)
            w = jnp.concatenate(weighed, axis=0)
            sel[way, q, d] = one.astype(BF16)
            if way == BWD:
                sum_w = jnp.sum(w, axis=1, keepdims=True)
                slot_w[q, d] = jnp.broadcast_to(sum_w, (SIDE * PAIR, 128))
                back = jnp.concatenate([one] + fill, axis=0).T
                sel_t[2, q, d] = back[:, : SIDE * PAIR].astype(BF16)
            else:
                back = jnp.concatenate([w] + fill, axis=0).T[:, : SIDE * PAIR]
                high = back.astype(BF16)
                sel_t[0, q, d] = high
                sel_t[1, q, d] = (back - high.astype(F32)).astype(BF16)

    def block(ref, q, a, b):
        return ref.at[a, b] if q == 1 else ref.at[b, a]

    def send_slots(t, q, d):
        way = FWD if t == HF else BWD
        for n in range(HALF // NT):
            cols = slice(n * NT, (n + 1) * NT)
            rows = dot(sel[way, q, d], dense[t, q, d, :, :, cols].reshape(2 * TOK, NT))
            if t == G:
                rows = rows * jnp.concatenate([slot_w[q, d]] * (NT // 128), axis=1)
            rows = rows.astype(BF16)
            block(slots.at[t, q], q, d, 0)[:, cols] = rows[:PAIR]
            pool[t, q, d, :, :, cols] = rows[PAIR:].reshape(SIDE - 1, PAIR, NT)
        for i in (2, 1, 3):
            there = block(slots.at[t, q], q, d, SIDE - i)
            send(pool.at[t, q, d, i - 1], there, xs.at[t], xr.at[t, q], second(q, i))

    def send_other_slots(t):
        @pl.loop(1, SIDE)
        def _(d):
            for q in (0, 1):
                for dz in (0, 1):
                    take(dense.at[t, q, d, dz], ds_r.at[t, q, d, dz])
                send_slots(t, q, d)

    send_partners(G)
    for q in (0, 1):
        send_slots(G, q, 0)
    send_own(HF)
    send_other_slots(G)
    send_partners(HB)
    for q in (0, 1):
        send_slots(HB, q, 0)
    send_other_slots(HB)
    send_partners(HF)
    for q in (0, 1):
        send_slots(HF, q, 0)
    send_other_slots(HF)

    for load in loads:
        load.wait()

    def arrived(t):
        for q in (0, 1):
            take(slots.at[t, q, 0:3], xr.at[t, q])

    def rows_of(t, q, h):
        return slots[t, q, pl.ds(2 * h, 2)].reshape(2 * SIDE * PAIR, HALF)

    def gate_up(t, h, n):
        cols = pl.ds(pl.multiple_of(n * NT, NT), NT)
        r0, r1 = rows_of(t, 0, h), rows_of(t, 1, h)
        a = dot(r0, wg[:HALF, cols]) + dot(r1, wg[HALF:, cols])
        u = dot(r0, wu[:HALF, cols]) + dot(r1, wu[HALF:, cols])
        return a, u, cols

    n_rows = 2 * SIDE * PAIR

    def send_back(way, make):
        for step in range(4):
            q, h = step % 2, 1 - step // 2

            @pl.loop(0, HALF // NT)
            def _(n, q=q, h=h):
                cols = pl.ds(pl.multiple_of(n * NT, NT), NT)
                made = make(q, h, n).astype(BF16)
                for k in range(2 * SIDE):
                    dx, dy = 2 * h + k // SIDE, k % SIDE
                    b, a = (dx, dy) if q == 0 else (dy, dx)
                    one = made[k * PAIR : (k + 1) * PAIR]
                    if b == 0:
                        ret[way, q, a, 0, :, cols] = one
                    else:
                        pool[way, q, a, b - 1, :, cols] = one

            for k in range(2 * SIDE):
                dx, dy = 2 * h + k // SIDE, k % SIDE
                b, a = (dx, dy) if q == 0 else (dy, dx)
                if b:
                    there = ret.at[way, q, a, SIDE - b]
                    send(pool.at[way, q, a, b - 1], there, rs.at[way], rr.at[way, q, a], second(q, b))

    arrived(G)
    arrived(HB)

    @pl.loop(0, 6)
    def _(step):
        h, n = step // 3, lax.rem(step, 3)
        a, u, cols = gate_up(HB, h, n)
        r0, r1 = rows_of(G, 0, h), rows_of(G, 1, h)
        dact = dot_t(r0, wd[cols, :HALF]) + dot_t(r1, wd[cols, HALF:])
        sg = jax.nn.sigmoid(a)
        rows = pl.ds(pl.multiple_of(h * n_rows, n_rows), n_rows)
        act1[rows, cols] = (dact * u * sg * (1.0 + a * (1.0 - sg))).astype(BF16)
        act2[rows, cols] = (dact * a * sg).astype(BF16)

    for t in (G, HB):
        take(pool.at[t], xs.at[t])

    def make_dh(q, h, n):
        rows = pl.ds(pl.multiple_of(q * HALF + n * NT, NT), NT)
        mine = slice(h * n_rows, (h + 1) * n_rows)
        return dot_t(act1[mine], wg[rows]) + dot_t(act2[mine], wu[rows])

    send_back(BWD, make_dh)
    arrived(HF)

    @pl.loop(0, 6)
    def _(step):
        h, n = step // 3, lax.rem(step, 3)
        a, u, cols = gate_up(HF, h, n)
        rows = pl.ds(pl.multiple_of(h * n_rows, n_rows), n_rows)
        act1[rows, cols] = (a * jax.nn.sigmoid(a) * u).astype(BF16)

    def make_o(q, h, n):
        cols = pl.ds(pl.multiple_of(q * HALF + n * NT, NT), NT)
        return dot(act1[h * n_rows : (h + 1) * n_rows], wd[:, cols])

    send_back(FWD, make_o)

    def combine(way, q, d):
        take(ret.at[way, q, d, 0:3], rr.at[way, q, d])
        for n in range(HALF // NT):
            cols = slice(n * NT, (n + 1) * NT)
            rows = ret[way, q, d, :, :, cols].reshape(SIDE * PAIR, NT)
            if way == BWD:
                total = dot(sel_t[2, q, d], rows)
            else:
                total = dot(sel_t[0, q, d], rows) + dot(sel_t[1, q, d], rows)
            if d == 0:
                own[q, :, cols] = total
            else:
                part[way, q, d - 1, :, cols] = total.astype(BF16)
        if d:
            there = gath.at[way, q, SIDE - d - 1]
            send(part.at[way, q, d - 1], there, cs.at[way], cr.at[way, q], first(q, d))

    def cross(way, q):
        take(gath.at[way, q], cr.at[way, q])
        total = own[q]
        for d in range(SIDE - 1):
            total = total + gath[way, q, d].astype(F32)
        zout[way, q] = total[TOK:].astype(BF16)
        send(zout.at[way, q], zin.at[way, q], qs.at[way, q], qr.at[way, q], partner)
        own[q, :TOK] = total[:TOK]

    def mixed(way, q):
        take(zin.at[way, q], qr.at[way, q])
        return own[q, :TOK] + zin[way, q].astype(F32)

    def gather(way):
        for d in (2, 1, 3, 0):
            for q in (0, 1):
                combine(way, q, d)
        for q in (0, 1):
            cross(way, q)

    gather(BWD)
    dn = jnp.concatenate([mixed(BWD, 0), mixed(BWD, 1)], axis=1)
    xb = xb_ref[...].astype(F32)
    scale = lax.rsqrt(jnp.mean(xb * xb, axis=-1, keepdims=True) + EPS)
    v = gain_ref[...].astype(F32) * dn
    inner = jnp.mean(xb * v, axis=-1, keepdims=True)
    dx = scale * v - xb * (scale * scale * scale) * inner
    last[BWD] = (gr_ref[...].astype(F32) + dx).astype(BF16)
    send(last.at[BWD], outb_ref, ps.at[BWD], pr.at[BWD], behind)
    gather(FWD)
    for q in (0, 1):
        cols = slice(q * HALF, (q + 1) * HALF)
        last[FWD, :, cols] = (xf_ref[:, cols].astype(F32) + mixed(FWD, q)).astype(BF16)
    send(last.at[FWD], outf_ref, ps.at[FWD], pr.at[FWD], ahead)

    take(outb_ref, pr.at[BWD])
    take(outf_ref, pr.at[FWD])
    take(meta_z, mz_s)
    take(meta_d.at[:, 1:4], ma_s)
    for t in (G, HB, HF):
        take(dense.at[t, :, 1:4], ds_s.at[t])
        for q in (0, 1):
            take(dense.at[t, q, 0, 0], zs.at[t, q])
    take(pool.at[HF], xs.at[HF])
    for way in (FWD, BWD):
        take(pool.at[way], rs.at[way])
        take(part.at[way], cs.at[way])
        for q in (0, 1):
            take(zout.at[way, q], qs.at[way, q])
        take(last.at[way], ps.at[way])


def local(*args):
    args = [a.reshape(a.shape[-2:]) for a in args]
    vm = pl.BlockSpec(memory_space=pltpu.VMEM)
    hbm = pl.BlockSpec(memory_space=pl.ANY)
    dma = pltpu.SemaphoreType.DMA
    out = jax.ShapeDtypeStruct((TOK, D), BF16)
    slots = (SIDE - 1, PAIR, HALF)
    got = pl.pallas_call(
        kernel,
        name="expert_layer",
        out_shape=(out, out),
        in_specs=[vm] * 8 + [hbm] * 3,
        out_specs=(vm, vm),
        scratch_shapes=[
            pltpu.VMEM((D, FF), BF16),
            pltpu.VMEM((D, FF), BF16),
            pltpu.VMEM((FF, D), BF16),
            pltpu.VMEM((3, 2, SIDE, 2, TOK, HALF), BF16),
            pltpu.VMEM((3, 2, SIDE) + slots, BF16),
            pltpu.VMEM((3, 2, SIDE, SIDE, PAIR, HALF), BF16),
            pltpu.VMEM((2, 2, SIDE, SIDE, PAIR, HALF), BF16),
            pltpu.VMEM((2, 2, SIDE - 1, 2 * TOK, HALF), BF16),
            pltpu.VMEM((2, 2 * TOK, HALF), F32),
            pltpu.VMEM((2, 2, SIDE - 1, 2 * TOK, HALF), BF16),
            pltpu.VMEM((2, 2, TOK, HALF), BF16),
            pltpu.VMEM((2, 2, TOK, HALF), BF16),
            pltpu.VMEM((2, TOK, D), BF16),
            pltpu.VMEM((SIDE * SIDE * PAIR, FF), BF16),
            pltpu.VMEM((SIDE * SIDE * PAIR, FF), BF16),
            pltpu.VMEM((2, 2, SIDE, 8, 128), F32),
            pltpu.VMEM((2, SIDE, 8, 128), F32),
            pltpu.VMEM((2, SIDE, 2, 8, 128), F32),
            pltpu.VMEM((2, 2, SIDE, SIDE * PAIR, 2 * TOK), BF16),
            pltpu.VMEM((3, 2, SIDE, 2 * TOK, SIDE * PAIR), BF16),
            pltpu.VMEM((2, SIDE, SIDE * PAIR, 128), F32),
            dma((3,)),
            dma,
            dma,
            dma,
            dma,
            dma((3, 2)),
            dma((3, 2)),
            dma((3,)),
            dma((3, 2, SIDE, 2)),
            dma((3,)),
            dma((3, 2)),
            dma((2,)),
            dma((2, 2, SIDE)),
            dma((2,)),
            dma((2, 2)),
            dma((2, 2)),
            dma((2, 2)),
            dma((2,)),
            dma((2,)),
        ],
        compiler_params=pltpu.CompilerParams(
            collective_id=0, has_side_effects=True, vmem_limit_bytes=62 * 1024 * 1000
        ),
        cost_estimate=pl.CostEstimate(
            flops=2 * 8 * 768 * D * FF, bytes_accessed=3 * 2 * D * FF, transcendentals=2 * 768 * FF
        ),
    )(*args)
    return tuple(o[None] for o in got)


def solution(mesh):
    rows = P("pipe", "ep", None)
    weights = P("pipe", "ep", None, None)
    return jax.shard_map(
        local,
        mesh=mesh,
        in_specs=(rows,) * 7 + (P("pipe", None),) + (weights,) * 3,
        out_specs=(rows, rows),
        check_vma=False,
    )
```

time: 489 us -> 200 us (0.41); the launches traced: 482 us -> 199 us
  Pallas kernels: 0 us -> 190 us
  starting transfers between devices: 151 us -> 0 us
  blocking collectives: 141 us -> 0 us
  waiting for transfers between devices: 57.2 us -> 0 us
  matrix products: 49.9 us -> 0 us
  local copies, waits for them, and re-layouts: 54.6 us -> 8.87 us
  other arithmetic: 27.2 us -> 0 us
    pallas_call x0 -> x1, Pallas kernels: none -> 190 us  [local(): pl.pallas_call(kernel, name='expert_layer', out_shape=(out, out), in_spec...]
    all_to_all x2 -> x0, blocking collectives: 141 us -> none  [the longest x1 72 us: local(): lax.all_to_all(send_f, 'ep', split_axis=0, concat_axis=0, tiled=True)]
    ppermute x2 -> x0, starting transfers between devices: 127 us -> none  [from_behind(): return lax.ppermute(block, axis, route)]
    all_to_all x3 -> x0, waiting for transfers between devices: 53.9 us -> none  [the longest x1 28.2 us: local(): lax.all_to_all(send_g, 'ep', split_axis=0, concat_axis=0, tiled=True)]
    dot_general x6 -> x0, matrix products: 49.9 us -> none  [the longest x1 12.7 us: expert_backward(): jnp.dot(dgate, w_g.T, preferred_element_type=jnp.float32)]
    gather x6 -> x0, local copies, waits for them, and re-layouts: 40.8 us -> none  [the longest x1 8.22 us: local(): send_b = jnp.where(valid_b, h_b[token_b], zero_b).reshape(n_exp, cap, width)]
    all_to_all x3 -> x0, starting transfers between devices: 24.4 us -> none  [the longest x1 14.3 us: local(): lax.all_to_all(made_b, 'ep', split_axis=0, concat_axis=0, tiled=True)]
    reduce_sum x9 -> x0, other arithmetic: 11.5 us -> none  [the longest x1 3.43 us: local(): jnp.sum(weights_f[:, :, None] * picked_f.astype(jnp.float32), axis=1)]
  transfers between devices with their start and end apart: 5 -> 0, of which waited for: 3 -> 0; matrix products, arithmetic and copies ran while one was open for 6% -> 0% of each run, Pallas kernels for 0% -> 0%
where the time goes in v1:
time: 200 us; the launch traced here: 199 us
  Pallas kernels  190 us (95%)
  local copies, waits for them, and re-layouts  8.87 us (4%)
    pallas_call x1, Pallas kernels, local(): pl.pallas_call(kernel, name='expert_layer', out_shape=(out, out), in_spec...  190 us
    unnamed x6, local copies, waits for them, and re-layouts  8.87 us

profile of v1, /device:TPU:1, one launch (start us, length us, event | category | flops | bytes accessed | tf_op | source)
XLA Modules:
  0.0 199.4 jit_solution(6554638780326860585)
XLA Ops:
  0.6 1.4 copy.13
  2.0 1.4 copy.14
  3.4 1.4 copy.15
  4.8 1.4 copy.16
  6.2 189.9 %expert_layer.1 = (bf16[64,2048]{1,0:T(8,128)(2,1)}, bf16[64,2048]{1,0:T(8,128)(2,1)}) custom-call(bf16[64,2048]{1,0:T(8,128)(2,1)} %bitcast.21, s32[64,8]{1,0:T(8,128)} %bitcast.14, f32[64,8]{1,0:T(8,128)} %bitcast.15, bf16[64,2048]{1,0:T(8,128)(2,1)} %bitcast.22, bf16[64,2048]{1,0:T(8,128)(2,1)} %bitcast.23, s32[64,8]{1,0:T(8,128)} %bitcast.16, ...), custom_call_target="tpu_custom_call" | custom-call | flops 19327352832 | bytes 9437184 | tf_op jit(solution)/shard_map/expert_layer/pallas_call | solution.py:366
  196.1 1.7 copy.19
  197.8 1.7 copy.20

commit v2 on v1

v2 whole, which is shorter than its diff:
```python
import functools

import jax
import jax.numpy as jnp
from jax import lax
from jax.experimental import pallas as pl
from jax.experimental.pallas import tpu as pltpu
from jax.sharding import PartitionSpec as P

EPS = 1e-06
MESH = pl.DeviceIdType.MESH
F32, BF16 = jnp.float32, jnp.bfloat16

SIDE = 4
TOK = 64
CAP = 24
PAIR = 2 * CAP
D = 2048
HALF = D // 2
CHUNKS = 4
WIDE = HALF // CHUNKS
FF = 768
TOP = 8
NT = 256
G, HB, HF = 0, 1, 2
FWD, BWD = 0, 1


def dot(a, b):
    return jnp.dot(a, b, preferred_element_type=F32)


def dot_t(a, b):
    return lax.dot_general(a, b, (((1,), (1,)), ((), ())), preferred_element_type=F32)


def kernel(
    xf_ref, idf_ref, rtf_ref, xb_ref, gr_ref, idb_ref, rtb_ref, gain_ref, wg_hbm, wu_hbm, wd_hbm,
    outf_ref, outb_ref,
    wg, wu, wd, dense, pool, slots, ret, part, own, gath, zout, zin, last, act1, act2,
    meta, meta_z, meta_d, sel, sel_t, slot_w,
    w_sem, mz_s, mz_r, ma_s, ma_r, zs, zr, ds_s, ds_r, xs, xr, rs, rr, cs, cr, qs, qr, ps, pr,
):
    p = lax.axis_index("pipe")
    e = lax.axis_index("ep")
    x, y, z = e // 8, lax.rem(e // 2, SIDE), lax.rem(e, 2)

    def at(dx, dy, dz):
        return (p, lax.rem(x + dx, SIDE) * 8 + lax.rem(y + dy, SIDE) * 2 + lax.rem(z + dz, 2))

    def first(q, d):
        return at(0, d, 0) if q == 0 else at(d, 0, 0)

    def second(q, d):
        return first(1 - q, d)

    partner = at(0, 0, 1)
    ahead, behind = (lax.rem(p + 1, 8), e), (lax.rem(p + 7, 8), e)

    def send(src, dst, s, r, device):
        pltpu.make_async_remote_copy(
            src_ref=src, dst_ref=dst, send_sem=s, recv_sem=r, device_id=device, device_id_type=MESH
        ).start()

    def take(ref, sem):
        pltpu.make_async_copy(ref, ref, sem).wait()

    barrier = pltpu.get_barrier_semaphore()
    for device in [partner, ahead, behind] + [first(q, d) for q in (0, 1) for d in (1, 2, 3)]:
        pl.semaphore_signal(barrier, inc=1, device_id=device, device_id_type=MESH)
    loads = [
        pltpu.make_async_copy(src, dst, w_sem.at[i])
        for i, (src, dst) in enumerate(((wg_hbm, wg), (wu_hbm, wu), (wd_hbm, wd)))
    ]
    for load in loads:
        load.start()

    def send_across(t, q):
        send(dense.at[t, q, 0, 0], dense.at[t, q, 0, 1], zs.at[t, q], zr.at[t, q], partner)

    def to_first(t, q, d, dz, to):
        there = dense.at[t, q, (d - to) % SIDE, dz]
        send(dense.at[t, q, d, dz], there, ds_s.at[t], ds_r.at[t, q, (d - to) % SIDE, dz], first(q, to))

    def send_own(t):
        for to in (1, 3):
            for q in (0, 1):
                to_first(t, q, 0, 0, to)

    def forward_own(t):
        for q in (0, 1):
            take(dense.at[t, q, 3, 0], ds_r.at[t, q, 3, 0])
            to_first(t, q, 3, 0, 1)

    def normed(ref, t):
        v = ref[...].astype(F32)
        scale = lax.rsqrt(jnp.mean(v * v, axis=-1, keepdims=True) + EPS)
        h = (v * scale * gain_ref[...].astype(F32)).astype(BF16)
        for q in (0, 1):
            dense[t, q, 0, 0] = h[:, q * HALF : (q + 1) * HALF]

    row = lax.broadcasted_iota(jnp.int32, (128, 128), 0)
    i, d, q, dz = row % 4, (row // 8) % 4, (row // 32) % 2, row // 64
    ex = jnp.where(q == 0, i, d)
    ey = jnp.where(q == 0, d, i)
    expert = ((x + ex) % SIDE) * 8 + ((y + ey) % SIDE) * 2 + (z + dz) % 2
    ids = jnp.concatenate([idf_ref[...], idb_ref[...]], axis=1)
    route = jnp.concatenate([rtf_ref[...], rtb_ref[...]], axis=1)
    route = route / jnp.sum(route, axis=0, keepdims=True)
    picked = jnp.zeros((128, 128), F32)
    weight = jnp.zeros((128, 128), F32)
    for k in range(TOP):
        hit = jnp.broadcast_to(ids[k : k + 1], (128, 128)) == expert
        picked = jnp.where(hit, 1.0, picked)
        weight = jnp.where(hit, jnp.broadcast_to(route[k : k + 1], (128, 128)), weight)
    early = lax.broadcasted_iota(jnp.int32, (128, 128), 0)
    late = lax.broadcasted_iota(jnp.int32, (128, 128), 1)
    order = jnp.where((early < late) & (early // TOK == late // TOK), 1.0, 0.0).astype(BF16)
    before = dot(picked.astype(BF16), order)
    place = jnp.where(picked > 0.0, before, -1000.0)
    kind = (row // 4) % 2
    meta[...] = jnp.where(kind == 0, place, weight).reshape(2, 2, 4, 8, 128)
    for q in (0, 1):
        dense[G, q, 0, 0] = gr_ref[:, q * HALF : (q + 1) * HALF]
    pl.semaphore_wait(barrier, 9)
    send(meta.at[1], meta_z, mz_s, mz_r, partner)
    for q in (0, 1):
        for d in (1, 2, 3):
            send(meta.at[0, q, d], meta_d.at[q, SIDE - d, 0], ma_s, ma_r, first(q, d))
    send_across(G, 0)
    send_across(G, 1)
    send_own(G)
    normed(xb_ref, HB)
    take(meta_z, mz_r)
    for q in (0, 1):
        for d in (1, 2, 3):
            send(meta_z.at[q, d], meta_d.at[q, SIDE - d, 1], ma_s, ma_r, first(q, d))
        meta_d[q, 0, 0] = meta[0, q, 0]
        meta_d[q, 0, 1] = meta_z[q, 0]
    send_across(HB, 0)
    send_across(HB, 1)
    send_own(HB)
    normed(xf_ref, HF)
    send_across(HF, 0)
    send_across(HF, 1)
    send_own(HF)
    forward_own(G)
    take(meta_d.at[:, 1:4], ma_r)

    lane = lax.broadcasted_iota(jnp.int32, (8, 128), 1)
    slot = lax.broadcasted_iota(jnp.int32, (PAIR, 128), 0).astype(F32)

    @pl.loop(0, 8)
    def _(n):
        q, d = n // 4, lax.rem(n, 4)
        m0, m1 = meta_d[q, d, 0], meta_d[q, d, 1]
        r0, r1 = pltpu.roll(m0, TOK, 1), pltpu.roll(m1, TOK, 1)
        for way, m in ((FWD, jnp.where(lane < TOK, m0, r1)), (BWD, jnp.where(lane < TOK, r0, m1))):
            shifted = m + jnp.where(lane < TOK, 0.0, 1.0 * CAP)
            ones, weighed = [], []
            for i in range(SIDE):
                hit = jnp.broadcast_to(shifted[i : i + 1], (PAIR, 128)) == slot
                ones.append(jnp.where(hit, 1.0, 0.0))
                weighed.append(jnp.where(hit, jnp.broadcast_to(m[4 + i : 5 + i], (PAIR, 128)), 0.0))
            fill = [jnp.zeros((256 - SIDE * PAIR, 128), F32)]
            one = jnp.concatenate(ones, axis=0)
            w = jnp.concatenate(weighed, axis=0)
            sel[way, q, d] = one.astype(BF16)
            if way == BWD:
                sum_w = jnp.sum(w, axis=1, keepdims=True)
                slot_w[q, d] = jnp.broadcast_to(sum_w, (SIDE * PAIR, 128))
                back = jnp.concatenate([one] + fill, axis=0).T
                sel_t[2, q, d] = back[:, : SIDE * PAIR].astype(BF16)
            else:
                back = jnp.concatenate([w] + fill, axis=0).T[:, : SIDE * PAIR]
                high = back.astype(BF16)
                sel_t[0, q, d] = high
                sel_t[1, q, d] = (back - high.astype(F32)).astype(BF16)

    def block(ref, q, a, b):
        return ref.at[a, b] if q == 1 else ref.at[b, a]

    def send_slots(t, d):
        way = FWD if t == HF else BWD
        for q in (0, 1):

            @pl.loop(0, HALF // NT)
            def _(n, q=q):
                cols = pl.ds(pl.multiple_of(n * NT, NT), NT)
                rows = dot(sel[way, q, d], dense[t, q, d, :, :, cols].reshape(2 * TOK, NT))
                if t == G:
                    rows = rows * jnp.concatenate([slot_w[q, d]] * (NT // 128), axis=1)
                rows = rows.astype(BF16)
                block(slots.at[t, q], q, d, 0)[:, cols] = rows[:PAIR]
                for k in range(1, SIDE):
                    pool[t, q, k, d, :, cols] = rows[k * PAIR : (k + 1) * PAIR]

        for i in (1, 3, 2):
            for q in (0, 1):
                there = block(slots.at[t, q], q, d, SIDE - i)
                send(pool.at[t, q, i, d], there, xs.at[t], xr.at[t, q], second(q, i))

    def near(t):
        for q in (0, 1):
            take(dense.at[t, q, 0, 1], zr.at[t, q])
            to_first(t, q, 0, 1, 3)
        for q in (0, 1):
            to_first(t, q, 0, 1, 1)
        send_slots(t, 0)

    def far(t):
        for q in (0, 1):
            take(dense.at[t, q, 1, 1], ds_r.at[t, q, 1, 1])
            to_first(t, q, 1, 1, 3)
        for d, news in ((3, (1,)), (1, (0,)), (2, (0, 1))):
            for dz in news:
                for q in (0, 1):
                    take(dense.at[t, q, d, dz], ds_r.at[t, q, d, dz])
            send_slots(t, d)

    near(G)
    forward_own(HB)
    forward_own(HF)
    far(G)
    near(HB)
    far(HB)
    near(HF)
    far(HF)

    for load in loads:
        load.wait()

    def arrived(t):
        for q in (0, 1):
            take(slots.at[t, q, 0:3], xr.at[t, q])

    def rows_of(t, q, h):
        return slots[t, q, pl.ds(2 * h, 2)].reshape(2 * SIDE * PAIR, HALF)

    def gate_up(t, h, n):
        cols = pl.ds(pl.multiple_of(n * NT, NT), NT)
        r0, r1 = rows_of(t, 0, h), rows_of(t, 1, h)
        a = dot(r0, wg[:HALF, cols]) + dot(r1, wg[HALF:, cols])
        u = dot(r0, wu[:HALF, cols]) + dot(r1, wu[HALF:, cols])
        return a, u, cols

    n_rows = 2 * SIDE * PAIR

    def chunk(c):
        return slice(c * WIDE, (c + 1) * WIDE)

    def send_back(way, c, make):
        for q in (0, 1):

            @pl.loop(0, 2 * (WIDE // NT))
            def _(step, q=q):
                h, n = lax.rem(step, 2), step // 2 + c * (WIDE // NT)
                cols = pl.ds(pl.multiple_of(n * NT, NT), NT)
                made = make(q, h, n).astype(BF16)
                for k in range(2 * SIDE):
                    one = made[k * PAIR : (k + 1) * PAIR]
                    if q == 0:
                        pool[way, q, 2 * h + k // SIDE, k % SIDE, :, cols] = one
                    else:
                        pool[way, q, k % SIDE, 2 * h + k // SIDE, :, cols] = one

        for d in range(SIDE):
            for b in (1, 3, 2):
                for q in (0, 1):
                    there = ret.at[way, q, SIDE - b, d, :, chunk(c)]
                    send(pool.at[way, q, b, d, :, chunk(c)], there, rs.at[way, c], rr.at[way, q, c], second(q, b))
        for q in (0, 1):
            ret[way, q, 0, :, :, chunk(c)] = pool[way, q, 0, :, :, chunk(c)]

    arrived(G)
    arrived(HB)

    @pl.loop(0, 6)
    def _(step):
        h, n = step // 3, lax.rem(step, 3)
        a, u, cols = gate_up(HB, h, n)
        r0, r1 = rows_of(G, 0, h), rows_of(G, 1, h)
        dact = dot_t(r0, wd[cols, :HALF]) + dot_t(r1, wd[cols, HALF:])
        sg = jax.nn.sigmoid(a)
        rows = pl.ds(pl.multiple_of(h * n_rows, n_rows), n_rows)
        act1[rows, cols] = (dact * u * sg * (1.0 + a * (1.0 - sg))).astype(BF16)
        act2[rows, cols] = (dact * a * sg).astype(BF16)

    for t in (G, HB):
        take(pool.at[t, :, 1:4], xs.at[t])

    def make_dh(q, h, n):
        rows = pl.ds(pl.multiple_of(q * HALF + n * NT, NT), NT)
        mine = pl.ds(pl.multiple_of(h * n_rows, n_rows), n_rows)
        return dot_t(act1[mine], wg[rows]) + dot_t(act2[mine], wu[rows])

    for c in range(CHUNKS):
        send_back(BWD, c, make_dh)
    arrived(HF)

    @pl.loop(0, 6)
    def _(step):
        h, n = step // 3, lax.rem(step, 3)
        a, u, cols = gate_up(HF, h, n)
        rows = pl.ds(pl.multiple_of(h * n_rows, n_rows), n_rows)
        act1[rows, cols] = (a * jax.nn.sigmoid(a) * u).astype(BF16)

    def make_o(q, h, n):
        cols = pl.ds(pl.multiple_of(q * HALF + n * NT, NT), NT)
        return dot(act1[pl.ds(pl.multiple_of(h * n_rows, n_rows), n_rows)], wd[:, cols])

    def combine(way, c):
        for q in (0, 1):
            take(ret.at[way, q, 1:4, :, :, chunk(c)], rr.at[way, q, c])
        for d in (1, 3, 2, 0):
            for q in (0, 1):
                for n in range(c * WIDE // NT, (c + 1) * WIDE // NT):
                    cols = slice(n * NT, (n + 1) * NT)
                    rows = jnp.concatenate([ret[way, q, i, d, :, cols] for i in range(SIDE)], axis=0)
                    if way == BWD:
                        total = dot(sel_t[2, q, d], rows)
                    else:
                        total = dot(sel_t[0, q, d], rows) + dot(sel_t[1, q, d], rows)
                    if d == 0:
                        own[way, q, :, cols] = total
                    else:
                        part[way, q, d - 1, :, cols] = total.astype(BF16)
                if d:
                    there = gath.at[way, q, SIDE - d - 1, :, chunk(c)]
                    send(part.at[way, q, d - 1, :, chunk(c)], there, cs.at[way], cr.at[way, q, c], first(q, d))

    def cross(way, c):
        cols = chunk(c)
        for q in (0, 1):
            take(gath.at[way, q, :, :, cols], cr.at[way, q, c])
            total = own[way, q, :, cols]
            for d in range(SIDE - 1):
                total = total + gath[way, q, d, :, cols].astype(F32)
            zout[way, q, :, cols] = total[TOK:].astype(BF16)
            send(zout.at[way, q, :, cols], zin.at[way, q, :, cols], qs.at[way], qr.at[way, q, c], partner)
            own[way, q, :TOK, cols] = total[:TOK]

    def crossed(way, q, c):
        cols = chunk(c)
        take(zin.at[way, q, :, cols], qr.at[way, q, c])
        return own[way, q, :TOK, cols] + zin[way, q, :, cols].astype(F32)

    def end_backward():
        dn = jnp.concatenate([crossed(BWD, q, c) for q in (0, 1) for c in range(CHUNKS)], axis=1)
        xb = xb_ref[...].astype(F32)
        scale = lax.rsqrt(jnp.mean(xb * xb, axis=-1, keepdims=True) + EPS)
        v = gain_ref[...].astype(F32) * dn
        inner = jnp.mean(xb * v, axis=-1, keepdims=True)
        dx = scale * v - xb * (scale * scale * scale) * inner
        last[BWD] = (gr_ref[...].astype(F32) + dx).astype(BF16)
        send(last.at[BWD], outb_ref, ps.at[BWD], pr.at[BWD], behind)

    def end_forward(c):
        for q in (0, 1):
            cols = slice(q * HALF + c * WIDE, q * HALF + (c + 1) * WIDE)
            last[FWD, :, cols] = (xf_ref[:, cols].astype(F32) + crossed(FWD, q, c)).astype(BF16)
            send(last.at[FWD, :, cols], outf_ref.at[:, cols], ps.at[FWD], pr.at[FWD], ahead)

    for c in range(CHUNKS):
        send_back(FWD, c, make_o)
        combine(BWD, c)
    for c in range(CHUNKS):
        cross(BWD, c)
        combine(FWD, c)
    end_backward()
    for c in range(CHUNKS):
        cross(FWD, c)
    for c in range(CHUNKS):
        end_forward(c)

    take(outb_ref, pr.at[BWD])
    take(outf_ref, pr.at[FWD])
    take(meta_z, mz_s)
    take(meta_d.at[:, 1:4], ma_s)
    for t in (G, HB, HF):
        take(dense.at[t, :, 1:4], ds_s.at[t])
        if t == HF:
            take(pool.at[t, :, 1:4], xs.at[t])
        for q in (0, 1):
            take(dense.at[t, q, 0, 0], zs.at[t, q])
    for way in (FWD, BWD):
        for c in range(CHUNKS):
            take(pool.at[way, :, 1:4, :, :, chunk(c)], rs.at[way, c])
        take(part.at[way], cs.at[way])
        take(zout.at[way], qs.at[way])
        take(last.at[way], ps.at[way])


def local(*args):
    args = [a.reshape(a.shape[-2:]) for a in args]
    for k in (1, 2, 5, 6):
        args[k] = args[k].T
    vm = pl.BlockSpec(memory_space=pltpu.VMEM)
    hbm = pl.BlockSpec(memory_space=pl.ANY)
    dma = pltpu.SemaphoreType.DMA
    out = jax.ShapeDtypeStruct((TOK, D), BF16)
    got = pl.pallas_call(
        kernel,
        name="expert_layer",
        out_shape=(out, out),
        in_specs=[vm] * 8 + [hbm] * 3,
        out_specs=(vm, vm),
        scratch_shapes=[
            pltpu.VMEM((D, FF), BF16),
            pltpu.VMEM((D, FF), BF16),
            pltpu.VMEM((FF, D), BF16),
            pltpu.VMEM((3, 2, SIDE, 2, TOK, HALF), BF16),
            pltpu.VMEM((3, 2, SIDE, SIDE, PAIR, HALF), BF16),
            pltpu.VMEM((3, 2, SIDE, SIDE, PAIR, HALF), BF16),
            pltpu.VMEM((2, 2, SIDE, SIDE, PAIR, HALF), BF16),
            pltpu.VMEM((2, 2, SIDE - 1, 2 * TOK, HALF), BF16),
            pltpu.VMEM((2, 2, 2 * TOK, HALF), F32),
            pltpu.VMEM((2, 2, SIDE - 1, 2 * TOK, HALF), BF16),
            pltpu.VMEM((2, 2, TOK, HALF), BF16),
            pltpu.VMEM((2, 2, TOK, HALF), BF16),
            pltpu.VMEM((2, TOK, D), BF16),
            pltpu.VMEM((SIDE * SIDE * PAIR, FF), BF16),
            pltpu.VMEM((SIDE * SIDE * PAIR, FF), BF16),
            pltpu.VMEM((2, 2, SIDE, 8, 128), F32),
            pltpu.VMEM((2, SIDE, 8, 128), F32),
            pltpu.VMEM((2, SIDE, 2, 8, 128), F32),
            pltpu.VMEM((2, 2, SIDE, SIDE * PAIR, 2 * TOK), BF16),
            pltpu.VMEM((3, 2, SIDE, 2 * TOK, SIDE * PAIR), BF16),
            pltpu.VMEM((2, SIDE, SIDE * PAIR, 128), F32),
            dma((3,)),
            dma,
            dma,
            dma,
            dma,
            dma((3, 2)),
            dma((3, 2)),
            dma((3,)),
            dma((3, 2, SIDE, 2)),
            dma((3,)),
            dma((3, 2)),
            dma((2, CHUNKS)),
            dma((2, 2, CHUNKS)),
            dma((2,)),
            dma((2, 2, CHUNKS)),
            dma((2,)),
            dma((2, 2, CHUNKS)),
            dma((2,)),
            dma((2,)),
        ],
        compiler_params=pltpu.CompilerParams(
            collective_id=0, has_side_effects=True, vmem_limit_bytes=62 * 1024 * 1000
        ),
        cost_estimate=pl.CostEstimate(
            flops=2 * 8 * 768 * D * FF, bytes_accessed=3 * 2 * D * FF, transcendentals=2 * 768 * FF
        ),
    )(*args)
    return tuple(o[None] for o in got)


def solution(mesh):
    rows = P("pipe", "ep", None)
    weights = P("pipe", "ep", None, None)
    return jax.shard_map(
        local,
        mesh=mesh,
        in_specs=(rows,) * 7 + (P("pipe", None),) + (weights,) * 3,
        out_specs=(rows, rows),
        check_vma=False,
    )
```

time: 200 us -> 175 us (0.88)
  the two profiles are of different devices: /device:TPU:1 before, /device:TPU:33 now
where the time goes in v2:
time: 175 us; the launch traced here: 174 us
  Pallas kernels  170 us (97%)
  local copies, waits for them, and re-layouts  3.34 us (2%)
    pallas_call x1, Pallas kernels, local(): pl.pallas_call(kernel, name='expert_layer', out_shape=(out, out), in_spec...  170 us

profile of v2, /device:TPU:33, one launch (start us, length us, event | category | flops | bytes accessed | tf_op | source)
XLA Modules:
  0.0 174.4 jit_solution(6625970599116482598)
XLA Ops:
  0.6 170.4 %expert_layer.1 = (bf16[64,2048]{1,0:T(8,128)(2,1)}, bf16[64,2048]{1,0:T(8,128)(2,1)}) custom-call(bf16[64,2048]{1,0:T(8,128)(2,1)} %bitcast.25, s32[8,64]{1,0:T(8,128)} %bitcast.28, f32[8,64]{1,0:T(8,128)} %bitcast.29, bf16[64,2048]{1,0:T(8,128)(2,1)} %bitcast.26, bf16[64,2048]{1,0:T(8,128)(2,1)} %bitcast.27, s32[8,64]{1,0:T(8,128)} %bitcast.30, ...), custom_call_target="tpu_custom_call" | custom-call | flops 19327352832 | bytes 9437184 | tf_op jit(solution)/shard_map/expert_layer/pallas_call | solution.py:402
  171.1 1.7 copy.15
  172.8 1.7 copy.16

commit v3 on v2

--- a/solution.py
+++ b/solution.py
@@ -37,9 +37,9 @@
 def kernel(
     xf_ref, idf_ref, rtf_ref, xb_ref, gr_ref, idb_ref, rtb_ref, gain_ref, wg_hbm, wu_hbm, wd_hbm,
     outf_ref, outb_ref,
-    wg, wu, wd, dense, pool, slots, ret, part, own, gath, zout, zin, last, act1, act2,
+    wg, wu, wd, dense, pool, slots, ret, part, held, via, own, gath, zout, zin, last, act1, act2,
     meta, meta_z, meta_d, sel, sel_t, slot_w,
-    w_sem, mz_s, mz_r, ma_s, ma_r, zs, zr, ds_s, ds_r, xs, xr, rs, rr, cs, cr, qs, qr, ps, pr,
+    w_sem, mz_s, mz_r, ma_s, ma_r, zs, zr, ds_s, ds_r, xs, xr, rs, rr, vr, cs, cr, qs, qr, ps, pr,
 ):
     p = lax.axis_index("pipe")
     e = lax.axis_index("ep")
@@ -87,10 +87,12 @@
             for q in (0, 1):
                 to_first(t, q, 0, 0, to)
 
-    def forward_own(t):
-        for q in (0, 1):
-            take(dense.at[t, q, 3, 0], ds_r.at[t, q, 3, 0])
-            to_first(t, q, 3, 0, 1)
+    def forward(t, dz):
+        for d, to, cols in ((3, 1, slice(0, HALF // 2)), (1, 3, slice(HALF // 2, HALF))):
+            for q in (0, 1):
+                take(dense.at[t, q, d, dz], ds_r.at[t, q, d, dz])
+                mine = dense.at[t, q, d, dz, :, cols]
+                send(mine, dense.at[t, q, 2, dz, :, cols], ds_s.at[t], ds_r.at[t, q, 2, dz], first(q, to))
 
     def normed(ref, t):
         v = ref[...].astype(F32)
@@ -137,14 +139,10 @@
             send(meta_z.at[q, d], meta_d.at[q, SIDE - d, 1], ma_s, ma_r, first(q, d))
         meta_d[q, 0, 0] = meta[0, q, 0]
         meta_d[q, 0, 1] = meta_z[q, 0]
-    send_across(HB, 0)
-    send_across(HB, 1)
     send_own(HB)
     normed(xf_ref, HF)
-    send_across(HF, 0)
-    send_across(HF, 1)
     send_own(HF)
-    forward_own(G)
+    forward(G, 0)
     take(meta_d.at[:, 1:4], ma_r)
 
     lane = lax.broadcasted_iota(jnp.int32, (8, 128), 1)
@@ -195,7 +193,7 @@
                 for k in range(1, SIDE):
                     pool[t, q, k, d, :, cols] = rows[k * PAIR : (k + 1) * PAIR]
 
-        for i in (1, 3, 2):
+        for i in (2, 1, 3):
             for q in (0, 1):
                 there = block(slots.at[t, q], q, d, SIDE - i)
                 send(pool.at[t, q, i, d], there, xs.at[t], xr.at[t, q], second(q, i))
@@ -203,24 +201,25 @@
     def near(t):
         for q in (0, 1):
             take(dense.at[t, q, 0, 1], zr.at[t, q])
+            if t < HF:
+                send_across(t + 1, q)
             to_first(t, q, 0, 1, 3)
         for q in (0, 1):
             to_first(t, q, 0, 1, 1)
         send_slots(t, 0)
 
     def far(t):
-        for q in (0, 1):
-            take(dense.at[t, q, 1, 1], ds_r.at[t, q, 1, 1])
-            to_first(t, q, 1, 1, 3)
-        for d, news in ((3, (1,)), (1, (0,)), (2, (0, 1))):
-            for dz in news:
-                for q in (0, 1):
-                    take(dense.at[t, q, d, dz], ds_r.at[t, q, d, dz])
-            send_slots(t, d)
+        forward(t, 1)
+        send_slots(t, 3)
+        send_slots(t, 1)
+        for q in (0, 1):
+            for dz in (0, 1):
+                take(dense.at[t, q, 2, dz], ds_r.at[t, q, 2, dz])
+        send_slots(t, 2)
 
     near(G)
-    forward_own(HB)
-    forward_own(HF)
+    forward(HB, 0)
+    forward(HF, 0)
     far(G)
     near(HB)
     far(HB)
@@ -312,7 +311,7 @@
     def combine(way, c):
         for q in (0, 1):
             take(ret.at[way, q, 1:4, :, :, chunk(c)], rr.at[way, q, c])
-        for d in (1, 3, 2, 0):
+        for d in (2, 1, 3, 0):
             for q in (0, 1):
                 for n in range(c * WIDE // NT, (c + 1) * WIDE // NT):
                     cols = slice(n * NT, (n + 1) * NT)
@@ -323,19 +322,43 @@
                         total = dot(sel_t[0, q, d], rows) + dot(sel_t[1, q, d], rows)
                     if d == 0:
                         own[way, q, :, cols] = total
+                    elif d == 1:
+                        held[way, q, 0, :, cols] = total[:TOK]
+                        part[way, q, 0, TOK:, cols] = total[TOK:].astype(BF16)
+                    elif d == 3:
+                        held[way, q, 1, :, cols] = total[TOK:]
+                        part[way, q, 2, :TOK, cols] = total[:TOK].astype(BF16)
                     else:
-                        part[way, q, d - 1, :, cols] = total.astype(BF16)
-                if d:
-                    there = gath.at[way, q, SIDE - d - 1, :, chunk(c)]
-                    send(part.at[way, q, d - 1, :, chunk(c)], there, cs.at[way], cr.at[way, q, c], first(q, d))
+                        part[way, q, 1, :, cols] = total.astype(BF16)
+            for q in (0, 1):
+                if d == 2:
+                    for k, to in ((0, 1), (1, 3)):
+                        mine = part.at[way, q, 1, k * TOK : (k + 1) * TOK, chunk(c)]
+                        send(mine, via.at[way, q, k, :, chunk(c)], cs.at[way], vr.at[way, q, c], first(q, to))
+                elif d:
+                    to_gath(way, q, c, d, 1 if d == 1 else 0)
+
+    def to_gath(way, q, c, d, k):
+        mine = part.at[way, q, d - 1, k * TOK : (k + 1) * TOK, chunk(c)]
+        there = gath.at[way, q, d // 2, k * TOK : (k + 1) * TOK, chunk(c)]
+        send(mine, there, cs.at[way], cr.at[way, q, c], first(q, d))
+
+    def relay(way, c):
+        cols = chunk(c)
+        for q in (0, 1):
+            take(via.at[way, q, :, :, cols], vr.at[way, q, c])
+            for k, d in ((0, 1), (1, 3)):
+                total = held[way, q, k, :, cols] + via[way, q, k, :, cols].astype(F32)
+                part[way, q, d - 1, k * TOK : (k + 1) * TOK, cols] = total.astype(BF16)
+                to_gath(way, q, c, d, k)
 
     def cross(way, c):
         cols = chunk(c)
         for q in (0, 1):
             take(gath.at[way, q, :, :, cols], cr.at[way, q, c])
             total = own[way, q, :, cols]
-            for d in range(SIDE - 1):
-                total = total + gath[way, q, d, :, cols].astype(F32)
+            for k in range(2):
+                total = total + gath[way, q, k, :, cols].astype(F32)
             zout[way, q, :, cols] = total[TOK:].astype(BF16)
             send(zout.at[way, q, :, cols], zin.at[way, q, :, cols], qs.at[way], qr.at[way, q, c], partner)
             own[way, q, :TOK, cols] = total[:TOK]
@@ -364,13 +387,27 @@
     for c in range(CHUNKS):
         send_back(FWD, c, make_o)
         combine(BWD, c)
+        if c:
+            relay(BWD, c - 1)
+        if c > 1:
+            cross(BWD, c - 2)
+    relay(BWD, CHUNKS - 1)
+    cross(BWD, CHUNKS - 2)
     for c in range(CHUNKS):
-        cross(BWD, c)
         combine(FWD, c)
-    end_backward()
-    for c in range(CHUNKS):
-        cross(FWD, c)
-    for c in range(CHUNKS):
+        if c == 0:
+            cross(BWD, CHUNKS - 1)
+        else:
+            relay(FWD, c - 1)
+        if c > 1:
+            cross(FWD, c - 2)
+        if c == 2:
+            end_backward()
+    relay(FWD, CHUNKS - 1)
+    cross(FWD, CHUNKS - 2)
+    end_forward(0)
+    cross(FWD, CHUNKS - 1)
+    for c in range(1, CHUNKS):
         end_forward(c)
 
     take(outb_ref, pr.at[BWD])
@@ -389,6 +426,11 @@
         take(part.at[way], cs.at[way])
         take(zout.at[way], qs.at[way])
         take(last.at[way], ps.at[way])
+
+
+def settle(f_ref, b_ref, outf_ref, outb_ref):
+    outf_ref[...] = f_ref[...]
+    outb_ref[...] = b_ref[...]
 
 
 def local(*args):
@@ -414,8 +456,10 @@
             pltpu.VMEM((3, 2, SIDE, SIDE, PAIR, HALF), BF16),
             pltpu.VMEM((2, 2, SIDE, SIDE, PAIR, HALF), BF16),
             pltpu.VMEM((2, 2, SIDE - 1, 2 * TOK, HALF), BF16),
+            pltpu.VMEM((2, 2, 2, TOK, HALF), F32),
+            pltpu.VMEM((2, 2, 2, TOK, HALF), BF16),
             pltpu.VMEM((2, 2, 2 * TOK, HALF), F32),
-            pltpu.VMEM((2, 2, SIDE - 1, 2 * TOK, HALF), BF16),
+            pltpu.VMEM((2, 2, 2, 2 * TOK, HALF), BF16),
             pltpu.VMEM((2, 2, TOK, HALF), BF16),
             pltpu.VMEM((2, 2, TOK, HALF), BF16),
             pltpu.VMEM((2, TOK, D), BF16),
@@ -440,6 +484,7 @@
             dma((3, 2)),
             dma((2, CHUNKS)),
             dma((2, 2, CHUNKS)),
+            dma((2, 2, CHUNKS)),
             dma((2,)),
             dma((2, 2, CHUNKS)),
             dma((2,)),
@@ -454,6 +499,9 @@
             flops=2 * 8 * 768 * D * FF, bytes_accessed=3 * 2 * D * FF, transcendentals=2 * 768 * FF
         ),
     )(*args)
+    got = pl.pallas_call(
+        settle, name="settle", out_shape=(out, out), in_specs=[vm] * 2, out_specs=(vm, vm)
+    )(*got)
     return tuple(o[None] for o in got)
 
 

time: 175 us -> 169 us (0.966)
  the two profiles are of different devices: /device:TPU:33 before, /device:TPU:1 now
where the time goes in v3:
time: 169 us
  Pallas kernels  169 us (100%)
    pallas_call x1, Pallas kernels, local(): pl.pallas_call(kernel, name='expert_layer', out_shape=(out, out), in_spec...  167 us

profile of v3, /device:TPU:1, one launch (start us, length us, event | category | flops | bytes accessed | tf_op | source)
XLA Modules:
  0.0 169.3 jit_solution(13872613721098823773)
XLA Ops:
  0.6 166.8 %expert_layer.1 = (bf16[64,2048]{1,0:T(8,128)(2,1)}, bf16[64,2048]{1,0:T(8,128)(2,1)}) custom-call(bf16[64,2048]{1,0:T(8,128)(2,1)} %bitcast.23, s32[8,64]{1,0:T(8,128)} %bitcast.28, f32[8,64]{1,0:T(8,128)} %bitcast.29, bf16[64,2048]{1,0:T(8,128)(2,1)} %bitcast.24, bf16[64,2048]{1,0:T(8,128)(2,1)} %bitcast.25, s32[8,64]{1,0:T(8,128)} %bitcast.30, ...), custom_call_target="tpu_custom_call" | custom-call | flops 19327352832 | bytes 9437184 | tf_op jit(solution)/shard_map/expert_layer/pallas_call | solution.py:444
  167.4 1.8 %settle.1 = (bf16[64,2048]{1,0:T(8,128)(2,1)}, bf16[64,2048]{1,0:T(8,128)(2,1)}) custom-call(bf16[64,2048]{1,0:T(8,128)(2,1)} %get-tuple-element.6.f_ref, bf16[64,2048]{1,0:T(8,128)(2,1)} %get-tuple-element.7.b_ref), custom_call_target="tpu_custom_call" | custom-call | tf_op jit(solution)/shard_map/settle/pallas_call | solution.py:502

commit v4 on v3

--- a/solution.py
+++ b/solution.py
@@ -140,9 +140,9 @@
         meta_d[q, 0, 0] = meta[0, q, 0]
         meta_d[q, 0, 1] = meta_z[q, 0]
     send_own(HB)
+    forward(G, 0)
     normed(xf_ref, HF)
     send_own(HF)
-    forward(G, 0)
     take(meta_d.at[:, 1:4], ma_r)
 
     lane = lax.broadcasted_iota(jnp.int32, (8, 128), 1)
@@ -217,9 +217,9 @@
                 take(dense.at[t, q, 2, dz], ds_r.at[t, q, 2, dz])
         send_slots(t, 2)
 
-    near(G)
     forward(HB, 0)
     forward(HF, 0)
+    near(G)
     far(G)
     near(HB)
     far(HB)

time: 169 us -> 167 us (0.988)
  Pallas kernels: 169 us -> 166 us
    pallas_call x1, Pallas kernels: 167 us -> 164 us  [local(): pl.pallas_call(kernel, name='expert_layer', out_shape=(out, out), in_spec...]
where the time goes in v4:
time: 167 us
  Pallas kernels  166 us (99%)
    pallas_call x1, Pallas kernels, local(): pl.pallas_call(kernel, name='expert_layer', out_shape=(out, out), in_spec...  164 us

profile of v4, /device:TPU:1, one launch (start us, length us, event | category | flops | bytes accessed | tf_op | source)
XLA Modules:
  0.0 166.9 jit_solution(17501715135267572986)
XLA Ops:
  0.6 164.4 %expert_layer.1 = (bf16[64,2048]{1,0:T(8,128)(2,1)}, bf16[64,2048]{1,0:T(8,128)(2,1)}) custom-call(bf16[64,2048]{1,0:T(8,128)(2,1)} %bitcast.23, s32[8,64]{1,0:T(8,128)} %bitcast.28, f32[8,64]{1,0:T(8,128)} %bitcast.29, bf16[64,2048]{1,0:T(8,128)(2,1)} %bitcast.24, bf16[64,2048]{1,0:T(8,128)(2,1)} %bitcast.25, s32[8,64]{1,0:T(8,128)} %bitcast.30, ...), custom_call_target="tpu_custom_call" | custom-call | flops 19327352832 | bytes 9437184 | tf_op jit(solution)/shard_map/expert_layer/pallas_call | solution.py:444
  165.0 1.8 %settle.1 = (bf16[64,2048]{1,0:T(8,128)(2,1)}, bf16[64,2048]{1,0:T(8,128)(2,1)}) custom-call(bf16[64,2048]{1,0:T(8,128)(2,1)} %get-tuple-element.6.f_ref, bf16[64,2048]{1,0:T(8,128)(2,1)} %get-tuple-element.7.b_ref), custom_call_target="tpu_custom_call" | custom-call | tf_op jit(solution)/shard_map/settle/pallas_call | solution.py:502

commit v5 on v4

--- a/solution.py
+++ b/solution.py
@@ -140,9 +140,10 @@
         meta_d[q, 0, 0] = meta[0, q, 0]
         meta_d[q, 0, 1] = meta_z[q, 0]
     send_own(HB)
+    normed(xf_ref, HF)
     forward(G, 0)
-    normed(xf_ref, HF)
     send_own(HF)
+    forward(HB, 0)
     take(meta_d.at[:, 1:4], ma_r)
 
     lane = lax.broadcasted_iota(jnp.int32, (8, 128), 1)
@@ -217,7 +218,6 @@
                 take(dense.at[t, q, 2, dz], ds_r.at[t, q, 2, dz])
         send_slots(t, 2)
 
-    forward(HB, 0)
     forward(HF, 0)
     near(G)
     far(G)

time: 167 us -> 166 us (level)
  no operation moved by 1% of the time
where the time goes in v5:
time: 166 us
  Pallas kernels  165 us (99%)
    pallas_call x1, Pallas kernels, local(): pl.pallas_call(kernel, name='expert_layer', out_shape=(out, out), in_spec...  163 us

profile of v5, /device:TPU:1, one launch (start us, length us, event | category | flops | bytes accessed | tf_op | source)
XLA Modules:
  0.0 165.8 jit_solution(11855354233131090832)
XLA Ops:
  0.6 163.4 %expert_layer.1 = (bf16[64,2048]{1,0:T(8,128)(2,1)}, bf16[64,2048]{1,0:T(8,128)(2,1)}) custom-call(bf16[64,2048]{1,0:T(8,128)(2,1)} %bitcast.23, s32[8,64]{1,0:T(8,128)} %bitcast.28, f32[8,64]{1,0:T(8,128)} %bitcast.29, bf16[64,2048]{1,0:T(8,128)(2,1)} %bitcast.24, bf16[64,2048]{1,0:T(8,128)(2,1)} %bitcast.25, s32[8,64]{1,0:T(8,128)} %bitcast.30, ...), custom_call_target="tpu_custom_call" | custom-call | flops 19327352832 | bytes 9437184 | tf_op jit(solution)/shard_map/expert_layer/pallas_call | solution.py:444
  164.0 1.8 %settle.1 = (bf16[64,2048]{1,0:T(8,128)(2,1)}, bf16[64,2048]{1,0:T(8,128)(2,1)}) custom-call(bf16[64,2048]{1,0:T(8,128)(2,1)} %get-tuple-element.6.f_ref, bf16[64,2048]{1,0:T(8,128)(2,1)} %get-tuple-element.7.b_ref), custom_call_target="tpu_custom_call" | custom-call | tf_op jit(solution)/shard_map/settle/pallas_call | solution.py:502
